TPU v7x, 512 devices: a whole 4x4x16 slice. The times are simulated.
512 devices in a mesh: ctx: 32 (over z, core), head: 16 (over x, y).
Axes of the slice: x: 4, y: 4, z: 16, core: 2. Of those that a mesh axis runs over, the one named last changes fastest.
Arguments:
- tokens_in: bfloat16 [8192, 8192], P('ctx', 'head'), may hold values from -6 to 6
- starts: int32 [8192], P('ctx'), may hold values from 0 to 1, as said below
- log_decay: float32 [128, 8192], P('head', 'ctx'), may hold values from -1 to 0
- b_proj: bfloat16 [8192, 128], P('ctx'), may hold values from -0.5 to 0.5
- c_proj: bfloat16 [8192, 128], P('ctx'), may hold values from -0.5 to 0.5
- out_grad: bfloat16 [8192, 8192], P('ctx', 'head'), may hold values from -1.5 to 1.5
- conv_weight: float32 [4, 8192], P(None, 'head'), may hold values from -3 to 3
- conv_bias: float32 [8192], P('head'), may hold values from -3 to 3
- skip_gain: float32 [128], P('head'), may hold values from 0.5 to 2
Outputs:
- in_grad: float32 [8192, 8192], P('ctx', 'head')
- b_grad: float32 [8192, 128], P(('ctx', 'head'))
- c_grad: float32 [8192, 128], P(('ctx', 'head'))
- decay_grad: float32 [128, 8192], P('head', 'ctx')
Inputs may be any that keep to these rules, and one draw needn't show every extreme that they name: starts is 0 at every position after 8192 // 8; it is 1 at one or more positions from 1 through 256.
All inputs are finite; a program needn't handle non-finite values.
Results may differ from a plain program's by a relative error of at most 0.003.
Values may be sent and summed in bfloat16 or wider, within the bound.
A program may use at most 64 MiB of HBM per device.

v0:
```python
import jax
import jax.numpy as jnp
from jax import lax
from jax.sharding import PartitionSpec as P

HEAD_DIM = 64
STATE = 128
TAPS = 4


highest = lax.Precision.HIGHEST


def from_behind(block, axis, distance):
    devices = range(lax.axis_size(axis))
    route = [(i - distance, i) for i in devices if i - distance in devices]
    return lax.ppermute(block, axis, route)


def silu_slope(value_entry):
    sigma = jax.nn.sigmoid(value_entry)
    return sigma * (1.0 + value_entry * (1.0 - sigma))


def block_setup(log_block, start_block):
    cum_decay = jnp.cumsum(log_block, axis=1)
    doc_count = jnp.cumsum(start_block)
    keep_in = (doc_count == 0).astype(jnp.float32)
    keep_out = (doc_count == doc_count[-1]).astype(jnp.float32)
    final_cum = cum_decay[:, -1:]
    weight_in = jnp.exp(cum_decay) * keep_in[None, :]
    weight_out = jnp.exp(final_cum - cum_decay) * keep_out[None, :]
    carry_factor = jnp.exp(final_cum[:, 0]) * keep_in[-1]
    return (cum_decay, doc_count, weight_in, weight_out, carry_factor)


def block_states(act_rows, grad_rows, b_block, c_block, weight_in, weight_out):
    scaled_b = weight_out[:, :, None] * b_block.astype(jnp.float32)[None, :, :]
    scaled_c = weight_in[:, :, None] * c_block.astype(jnp.float32)[None, :, :]
    state_local = jnp.einsum(
        "htn,thp->hnp", scaled_b, act_rows.astype(jnp.float32), precision=highest
    )
    adjoint_local = jnp.einsum(
        "htn,thp->hnp", scaled_c, grad_rows.astype(jnp.float32), precision=highest
    )
    return (state_local, adjoint_local)


def intra_heads(act_heads, grad_heads, cum_decay, doc_count, scores):
    positions = jnp.arange(scores.shape[0])
    lower = (positions[:, None] >= positions[None, :]) & (doc_count[:, None] == doc_count[None, :])

    def one_head(total, inputs):
        act_head, grad_head, cum_head = inputs
        diff = cum_head[:, None] - cum_head[None, :]
        decay = jnp.where(lower, jnp.exp(jnp.minimum(diff, 0.0)), 0.0)
        mixed = decay * scores
        grad_wide = grad_head.astype(jnp.float32)
        act_grad = lax.dot_general(mixed, grad_wide, (((0,), (0,)), ((), ())), precision=highest)
        inner = lax.dot_general(
            grad_head, act_head, (((1,), (1,)), ((), ())), preferred_element_type=jnp.float32
        )
        total = total + decay * inner
        product = mixed * inner
        cum_grad = jnp.sum(product, axis=1) - jnp.sum(product, axis=0)
        return (total, (act_grad, cum_grad))

    return lax.scan(one_head, jnp.zeros_like(scores), (act_heads, grad_heads, cum_decay))


def inter_terms(
    act_rows,
    grad_rows,
    b_block,
    c_block,
    weight_in,
    weight_out,
    carry_factor,
    state_local,
    state_in,
    adjoint_in,
):
    act_wide = act_rows.astype(jnp.float32)
    grad_wide = grad_rows.astype(jnp.float32)
    from_after = jnp.einsum(
        "tn,hnp->thp", b_block.astype(jnp.float32), adjoint_in, precision=highest
    )
    from_before = jnp.einsum(
        "tn,hnp->thp", c_block.astype(jnp.float32), state_in, precision=highest
    )
    act_extra = weight_out.T[:, :, None] * from_after
    cum_extra = (
        weight_in * jnp.sum(from_before * grad_wide, axis=2).T
        - weight_out * jnp.sum(from_after * act_wide, axis=2).T
    )
    state_out = state_local + carry_factor[:, None, None] * state_in
    end_term = jnp.sum(adjoint_in * state_out, axis=(1, 2))
    is_last = (jnp.arange(weight_in.shape[1]) == weight_in.shape[1] - 1).astype(jnp.float32)
    cum_extra = cum_extra + end_term[:, None] * is_last[None, :]
    b_extra = jnp.einsum(
        "thp,hnp->tn", act_wide * weight_out.T[:, :, None], adjoint_in, precision=highest
    )
    c_extra = jnp.einsum(
        "thp,hnp->tn", grad_wide * weight_in.T[:, :, None], state_in, precision=highest
    )
    return (act_extra, cum_extra, b_extra, c_extra)


def body(tokens_in, starts, log_decay, b_proj, c_proj, out_grad, conv_weight, conv_bias, skip_gain):
    rows_here, channels = tokens_in.shape
    head_count = log_decay.shape[0]
    margin = TAPS - 1
    cum_decay, doc_count, weight_in, weight_out, carry_factor = block_setup(log_decay, starts)
    last_count = doc_count[rows_here - 1]
    tail_keep = (doc_count[rows_here - margin :] == last_count).astype(jnp.bfloat16)
    tail_rows = tokens_in[rows_here - margin :] * tail_keep[:, None]
    previous = from_behind(tail_rows, "ctx", 1)
    extended = jnp.concatenate([previous, tokens_in], axis=0).astype(jnp.float32)
    count_before = jnp.concatenate([jnp.zeros((margin,), jnp.int32), doc_count])
    pre_act = conv_bias[None, :] + conv_weight[0][None, :] * extended[margin:]
    for offset in range(1, TAPS):
        valid_mask = (
            doc_count == count_before[margin - offset : margin - offset + rows_here]
        ).astype(jnp.float32)
        pre_act = (
            pre_act
            + conv_weight[offset][None, :]
            * extended[margin - offset : margin - offset + rows_here]
            * valid_mask[:, None]
        )
    activated = jax.nn.silu(pre_act).astype(jnp.bfloat16)
    act_rows = activated.reshape(rows_here, head_count, HEAD_DIM)
    grad_rows = out_grad.reshape(rows_here, head_count, HEAD_DIM)
    state_local, adjoint_local = block_states(
        act_rows, grad_rows, b_proj, c_proj, weight_in, weight_out
    )
    gathered_factor, gathered_state, gathered_adjoint = (
        lax.all_gather(carry_factor[None], "ctx", axis=0, tiled=True),
        lax.all_gather(state_local[None], "ctx", axis=0, tiled=True),
        lax.all_gather(adjoint_local[None], "ctx", axis=0, tiled=True),
    )
    device_index = lax.axis_index("ctx")
    device_total = gathered_factor.shape[0]

    def forward_step(counter, state):
        updated = gathered_state[counter] + gathered_factor[counter][:, None, None] * state
        return jnp.where(counter < device_index, updated, state)

    def backward_step(counter, adjoint):
        source = device_total - 1 - counter
        updated = gathered_adjoint[source] + gathered_factor[source][:, None, None] * adjoint
        return jnp.where(source > device_index, updated, adjoint)

    state_in = lax.fori_loop(0, device_total, forward_step, jnp.zeros_like(state_local))
    adjoint_in = lax.fori_loop(0, device_total, backward_step, jnp.zeros_like(adjoint_local))
    scores = lax.dot_general(
        c_proj, b_proj, (((1,), (1,)), ((), ())), preferred_element_type=jnp.float32
    )
    score_grad, (heads_grad, cum_grad) = intra_heads(
        act_rows.transpose(1, 0, 2), grad_rows.transpose(1, 0, 2), cum_decay, doc_count, scores
    )
    act_extra, cum_extra, b_extra, c_extra = inter_terms(
        act_rows,
        grad_rows,
        b_proj,
        c_proj,
        weight_in,
        weight_out,
        carry_factor,
        state_local,
        state_in,
        adjoint_in,
    )
    act_total = (
        heads_grad.transpose(1, 0, 2)
        + act_extra
        + skip_gain[None, :, None] * grad_rows.astype(jnp.float32)
    )
    pre_grad = act_total.reshape(rows_here, channels) * silu_slope(pre_act)
    head_keep = (doc_count[:margin] == 0).astype(jnp.float32)
    head_rows = pre_grad[:margin] * head_keep[:, None]
    following = from_behind(head_rows, "ctx", -1)
    extended_grad = jnp.concatenate([pre_grad, following], axis=0)
    count_after = jnp.concatenate([doc_count, jnp.full((margin,), last_count, jnp.int32)])
    in_grad = conv_weight[0][None, :] * pre_grad
    for offset in range(1, TAPS):
        valid_mask = (count_after[offset : offset + rows_here] == doc_count).astype(jnp.float32)
        in_grad = (
            in_grad
            + conv_weight[offset][None, :]
            * extended_grad[offset : offset + rows_here]
            * valid_mask[:, None]
        )
    b_wide = b_proj.astype(jnp.float32)
    c_wide = c_proj.astype(jnp.float32)
    b_local = (
        lax.dot_general(score_grad, c_wide, (((0,), (0,)), ((), ())), precision=highest) + b_extra
    )
    c_local = jnp.dot(score_grad, b_wide, precision=highest) + c_extra
    shares = lax.psum_scatter(
        jnp.concatenate([b_local, c_local], axis=1), "head", scatter_dimension=0, tiled=True
    )
    cum_total = cum_grad + cum_extra
    decay_grad = jnp.flip(jnp.cumsum(jnp.flip(cum_total, axis=1), axis=1), axis=1)
    return (in_grad, shares[:, :STATE], shares[:, STATE:], decay_grad)


def solution(mesh):
    placed = (
        P("ctx", "head"),
        P("ctx"),
        P("head", "ctx"),
        P("ctx", None),
        P("ctx", None),
        P("ctx", "head"),
        P(None, "head"),
        P("head"),
        P("head"),
    )
    return jax.shard_map(
        body,
        mesh=mesh,
        in_specs=placed,
        out_specs=(
            P("ctx", "head"),
            P(("ctx", "head"), None),
            P(("ctx", "head"), None),
            P("head", "ctx"),
        ),
        check_vma=False,
    )
```

profile of v0, /device:TPU:1, one launch (start us, length us, event | category | flops | bytes accessed | tf_op | source)
XLA Modules:
  0.0 349.6 jit_solution(11958066550004650929)
XLA Ops:
  8.5 1.2 reduce-window.21
  9.9 1.1 copy.43
  12.6 1.4 fusion.28
  14.6 1.2 compare_convert_fusion.4
  16.6 4.9 %collective-permute-start = (bf16[3,512]{1,0:T(4,128)(2,1)S(1)}, bf16[3,512]{1,0:T(4,128)(2,1)S(1)}, u32[]{:S(2)}, u32[]{:S(2)}) collective-permute-start(bf16[3,512]{1,0:T(4,128)(2,1)S(1)} %slice_multiply_fusion.5), channel_id=1, source_target_pairs={{0,16},{16,32},{32,48},{48,64},{64,80},{80,96},{96,112},{112,128},... | collective-permute-start | bytes 9224 | tf_op jit(solution)/shard_map/ppermute | solution.py:17
  22.9 1.2 exponential_multiply_fusion.2
  24.1 1.3 compare_convert_fusion.3
  26.5 1.1 fusion.65
  29.0 1.3 dynamic-slice
  31.2 52.1 %all-reduce.2 = f32[256]{0:T(256)S(1)} all-reduce(f32[256]{0:T(256)S(1)} %dynamic-update-slice), channel_id=3, replica_groups=mesh['ctx'=32,'head'=16] {'ctx'}, use_global_device_ids=true, to_apply=%add.2 | all-reduce | flops 256 | bytes 2048
  83.4 1.0 maximum_convert_fusion
  84.4 1.1 multiply_convert_fusion
  85.7 1.4 fusion.26
  87.1 21.6 %while.45 = (s32[]{:T(128)}, f32[256,256]{1,0:T(8,128)S(1)}, f32[8,256,64]{1,2,0:T(8,128)}, f32[8,256]{1,0:T(8,128)}, f32[8,256]{1,0:T(8,128)S(1)}, /*index=5*/b...) while((s32[]{:T(128)}, f32[256,256]{1,0:T(8,128)S(1)}, ...), condition=%wide.region_7.8_spmd.clone, body=%wide.region_4.7_spmd.clone.sunk | while | flops 60030720 | bytes 1756287 | solution.py:68
  87.5 1.3 dynamic_update_slice.14
  90.2 1.3 dynamic_update_slice.14
  92.9 1.3 dynamic_update_slice.14
  95.6 1.3 dynamic_update_slice.14
  98.3 1.3 dynamic_update_slice.14
  101.0 1.3 dynamic_update_slice.14
  103.7 1.3 dynamic_update_slice.14
  106.4 1.3 dynamic_update_slice.14
  108.8 44.1 %while.46 = (s32[]{:T(128)}, f32[8,128,64]{2,1,0:T(8,128)S(1)}, s32[]{:T(128)}, f32[32,8,128,64]{2,3,1,0:T(8,128)}, f32[32,8]{1,0:T(8,128)S(1)}, /*index=5*/s32[]{:T(128)}, s32[]{:T(128)}, s32[]{:T(128)}, s32[]{:T(128)}) while((s32[]{:T(128)}, f32[8,128,64]{2,1,0:T(8,128)S(1)}, s32[]{:T(128)}, f32[32,8,128,64]{2,3,1,0:T(8,128)}, ...), condition=%wide.region_9.10_spmd.clone, body=%wide.region_8.9_spmd.clone.sunk | while | flops 262152 | bytes 1835271 | solution.py:155
  140.5 1.0 constant_dynamic-slice_fusion.7
  143.3 1.0 constant_dynamic-slice_fusion.7
  153.8 2.3 fusion.30
  157.3 4.1 %collective-permute-start.1 = (f32[3,512]{1,0:T(4,128)S(1)}, f32[3,512]{1,0:T(4,128)S(1)}, u32[]{:S(2)}, u32[]{:S(2)}) collective-permute-start(f32[3,512]{1,0:T(4,128)S(1)} %slice_multiply_fusion.4), channel_id=1, source_target_pairs={{16,0},{32,16},{48,32},{64,48},{80,64},{96,80},{112,96},{128,112},... | collective-permute-start | bytes 18440 | tf_op jit(solution)/shard_map/ppermute | solution.py:17
  162.4 28.1 %all-gather.8.cloned.1.call-done = f32[256,128,64]{1,2,0:T(8,128)} async-done(((f32[8,128,64]{1,2,0:T(8,128)}), f32[256,128,64]{1,2,0:T(8,128)}) %all-gather.8.cloned.1.call-update) | async-done | bytes 8388624 | tf_op jit(solution)/shard_map/all_gather | solution.py:139
  190.6 64.9 %while.47 = (s32[]{:T(128)}, f32[8,128,64]{2,1,0:T(8,128)S(1)}, s32[]{:T(128)}, f32[32,8,128,64]{2,3,1,0:T(8,128)}, f32[32,8]{1,0:T(8,128)}, /*index=5*/s32[]{:T(128)}, s32[]{:T(128)}) while((s32[]{:T(128)}, f32[8,128,64]{2,1,0:T(8,128)S(1)}, s32[]{:T(128)}, f32[32,8,128,64]{2,3,1,0:T(8,128)}, f32[32,8]{1,0:T(8,128)}, ...), condition=%wide.region_11.12_spmd.clone, body=%wide.region_10.11_spmd.clone.sunk | while | flops 262148 | bytes 1835209 | solution.py:154
  261.0 1.1 fusion.35
  262.1 79.6 %reduce-scatter.4.cloned.1.call-done = f32[16,256]{1,0:T(8,128)} async-done(((f32[256,256]{1,0:T(8,128)}), f32[16,256]{1,0:T(8,128)}) %reduce-scatter.4.cloned.1.call-update) | async-done | bytes 16400
  341.8 1.3 fusion.63
  (404 shorter events, 132.5 us)
Async XLA Ops:
  7.2 101.6 %all-gather.6.cloned.1.call-start = ((), (), s32[]{:S(2)}) async-start(), calls=%async_computation.1 | async-start | bytes 8650752 | tf_op jit(solution)/shard_map/all_gather | solution.py:140
  12.0 0.6 copy-start.4
  14.0 176.5 %all-gather.8.cloned.1.call-start = ((), (), s32[]{:S(2)}) async-start(), calls=%async_computation.2 | async-start | bytes 8650752 | tf_op jit(solution)/shard_map/all_gather | solution.py:139
  16.6 66.8 %collective-permute-start = (bf16[3,512]{1,0:T(4,128)(2,1)S(1)}, bf16[3,512]{1,0:T(4,128)(2,1)S(1)}, u32[]{:S(2)}, u32[]{:S(2)}) collective-permute-start(bf16[3,512]{1,0:T(4,128)(2,1)S(1)} %slice_multiply_fusion.5), channel_id=1, source_target_pairs={{0,16},{16,32},{32,48},{48,64},{64,80},{80,96},{96,112},{112,128},... | collective-permute-start | bytes 9224 | tf_op jit(solution)/shard_map/ppermute | solution.py:17
  22.9 64.1 %copy-start.18 = (f32[8]{0:T(128)}, f32[8]{0:T(128)S(1)}, u32[]{:S(2)}) copy-start(f32[8]{0:T(128)S(1)} %get-tuple-element.424) | copy-start | bytes 100
  25.4 61.7 %copy-start.15 = (f32[256]{0:T(256)}, f32[256]{0:T(256)S(1)}, u32[]{:S(2)}) copy-start(f32[256]{0:T(256)S(1)} %get-tuple-element.482) | copy-start | bytes 3076
  26.3 60.8 %copy-start.7 = (f32[1,512]{1,0:T(1,128)}, f32[1,512]{1,0:T(1,128)S(1)}, u32[]{:S(2)}) copy-start(f32[1,512]{1,0:T(1,128)S(1)} %get-tuple-element.476) | copy-start | bytes 6148
  26.3 60.8 %copy-start.9 = (f32[1,512]{1,0:T(1,128)}, f32[1,512]{1,0:T(1,128)S(1)}, u32[]{:S(2)}) copy-start(f32[1,512]{1,0:T(1,128)S(1)} %get-tuple-element.477) | copy-start | bytes 6148
  26.3 60.8 %copy-start.11 = (f32[1,512]{1,0:T(1,128)}, f32[1,512]{1,0:T(1,128)S(1)}, u32[]{:S(2)}) copy-start(f32[1,512]{1,0:T(1,128)S(1)} %get-tuple-element.478) | copy-start | bytes 6148
  26.3 60.8 %copy-start.13 = (f32[1,512]{1,0:T(1,128)}, f32[1,512]{1,0:T(1,128)S(1)}, u32[]{:S(2)}) copy-start(f32[1,512]{1,0:T(1,128)S(1)} %get-tuple-element.479) | copy-start | bytes 6148
  108.7 45.1 %copy-start.1 = (bf16[256,128]{1,0:T(8,128)(2,1)S(1)}, bf16[256,128]{1,0:T(8,128)(2,1)}, u32[]{:S(2)}) copy-start(bf16[256,128]{1,0:T(8,128)(2,1)} %param.18) | copy-start | bytes 196612
  108.7 45.1 %copy-start.24 = (f32[8]{0:T(128)S(1)}, f32[8]{0:T(128)}, u32[]{:S(2)}) copy-start(f32[8]{0:T(128)} %param.23) | copy-start | bytes 100
  108.7 233.0 %reduce-scatter.4.cloned.1.call-start = ((), (), s32[]{:S(2)}) async-start(), calls=%async_computation.3 | async-start | bytes 278528
  108.8 53.2 %copy-start.3 = (bf16[256,128]{1,0:T(8,128)(2,1)S(1)}, bf16[256,128]{1,0:T(8,128)(2,1)}, u32[]{:S(2)}) copy-start(bf16[256,128]{1,0:T(8,128)(2,1)} %param.19) | copy-start | bytes 196612
  152.9 3.2 copy-start.17
  157.3 103.7 %collective-permute-start.1 = (f32[3,512]{1,0:T(4,128)S(1)}, f32[3,512]{1,0:T(4,128)S(1)}, u32[]{:S(2)}, u32[]{:S(2)}) collective-permute-start(f32[3,512]{1,0:T(4,128)S(1)} %slice_multiply_fusion.4), channel_id=1, source_target_pairs={{16,0},{32,16},{48,32},{64,48},{80,64},{96,80},{112,96},{128,112},... | collective-permute-start | bytes 18440 | tf_op jit(solution)/shard_map/ppermute | solution.py:17
  162.1 94.3 %copy-start = (f32[8,128,64]{1,2,0:T(8,128)S(1)}, f32[8,128,64]{1,2,0:T(8,128)}, u32[]{:S(2)}) copy-start(f32[8,128,64]{1,2,0:T(8,128)} %copy.55) | copy-start | bytes 786436
  162.1 94.3 %copy-start.2 = (f32[8,128,64]{1,2,0:T(8,128)S(1)}, f32[8,128,64]{1,2,0:T(8,128)}, u32[]{:S(2)}) copy-start(f32[8,128,64]{1,2,0:T(8,128)} %fusion.26) | copy-start | bytes 786436
  162.1 94.3 %copy-start.25 = (f32[8]{0:T(128)S(1)}, f32[8]{0:T(128)}, u32[]{:S(2)}) copy-start(f32[8]{0:T(128)} %exponential_multiply_fusion.2) | copy-start | bytes 100
  190.5 66.1 %copy-start.5 = (f32[8,256]{1,0:T(8,128)S(1)}, f32[8,256]{1,0:T(8,128)}, u32[]{:S(2)}) copy-start(f32[8,256]{1,0:T(8,128)} %copy-done.4) | copy-start | bytes 24580
  190.5 66.1 %copy-start.6 = (f32[256,8]{0,1:T(8,128)S(1)}, f32[256,8]{0,1:T(8,128)}, u32[]{:S(2)}) copy-start(f32[256,8]{0,1:T(8,128)} %get-tuple-element.472) | copy-start | bytes 24580
  190.5 66.1 %copy-start.16 = (f32[256]{0:T(256)S(1)}, f32[256]{0:T(256)}, u32[]{:S(2)}) copy-start(f32[256]{0:T(256)} %copy-done.15) | copy-start | bytes 3076
  190.5 66.1 %copy-start.19 = (f32[8]{0:T(128)S(1)}, f32[8]{0:T(128)}, u32[]{:S(2)}) copy-start(f32[8]{0:T(128)} %copy-done.18) | copy-start | bytes 100
  190.5 66.1 %copy-start.23 = (f32[256]{0:T(256)S(1)}, f32[256]{0:T(256)}, u32[]{:S(2)}) copy-start(f32[256]{0:T(256)} %compare_convert_fusion) | copy-start | bytes 3076
  190.5 70.5 %copy-start.8 = (f32[1,512]{1,0:T(1,128)S(1)}, f32[1,512]{1,0:T(1,128)}, u32[]{:S(2)}) copy-start(f32[1,512]{1,0:T(1,128)} %copy-done.7) | copy-start | bytes 6148
  190.5 70.4 %copy-start.10 = (f32[1,512]{1,0:T(1,128)S(1)}, f32[1,512]{1,0:T(1,128)}, u32[]{:S(2)}) copy-start(f32[1,512]{1,0:T(1,128)} %copy-done.9) | copy-start | bytes 6148
  190.5 70.4 %copy-start.12 = (f32[1,512]{1,0:T(1,128)S(1)}, f32[1,512]{1,0:T(1,128)}, u32[]{:S(2)}) copy-start(f32[1,512]{1,0:T(1,128)} %copy-done.11) | copy-start | bytes 6148
  190.6 70.4 %copy-start.14 = (f32[1,512]{1,0:T(1,128)S(1)}, f32[1,512]{1,0:T(1,128)}, u32[]{:S(2)}) copy-start(f32[1,512]{1,0:T(1,128)} %copy-done.13) | copy-start | bytes 6148
  190.6 70.4 %copy-start.20 = (f32[256]{0:T(256)S(1)}, f32[256]{0:T(256)}, u32[]{:S(2)}) copy-start(f32[256]{0:T(256)} %get-tuple-element.480) | copy-start | bytes 3076
  190.6 70.4 %copy-start.21 = (f32[256]{0:T(256)S(1)}, f32[256]{0:T(256)}, u32[]{:S(2)}) copy-start(f32[256]{0:T(256)} %get-tuple-element.481) | copy-start | bytes 3076
  190.6 70.4 %copy-start.22 = (f32[256]{0:T(256)S(1)}, f32[256]{0:T(256)}, u32[]{:S(2)}) copy-start(f32[256]{0:T(256)} %get-tuple-element.486) | copy-start | bytes 3076
Sparse Core Ops, SparseCore 0:
  14.1 85.1 all-gather.5
  108.9 81.5 all-gather.7
  260.1 81.6 reduce-scatter.3
where the time goes:
time: 354 us; the launch traced here: 350 us
  local copies, waits for them, and re-layouts  119 us (34%)
  waiting for transfers between devices  108 us (31%)
  blocking collectives  52.1 us (15%)
  other arithmetic  25.7 us (7%)
  matrix products  18.6 us (5%)
  between operations  14.9 us (4%)
  starting transfers between devices  9.16 us (3%)
    unnamed x4, waiting for transfers between devices  79.7 us
    unnamed x1, blocking collectives  52.1 us
    dynamic_slice x64, local copies, waits for them, and re-layouts, backward_step(): gathered_adjoint[source] + gathered_factor[source][:, None, None] * adjoint  37.7 us
    dynamic_slice x64, local copies, waits for them, and re-layouts, forward_step(): gathered_state[counter] + gathered_factor[counter][:, None, None] * state  37.5 us
    all_gather x1, waiting for transfers between devices, body(): lax.all_gather(state_local[None], 'ctx', axis=0, tiled=True)  28.1 us
    mul x32, local copies, waits for them, and re-layouts, forward_step(): gathered_factor[counter][:, None, None] * state  22.1 us
    dynamic_update_slice x8, local copies, waits for them, and re-layouts, intra_heads(): lax.scan(one_head, jnp.zeros_like(scores), (act_heads, grad_heads, cum_de...  10.5 us
    ppermute x2, starting transfers between devices, from_behind(): return lax.ppermute(block, axis, route)  9.04 us
  transfers between devices with their start and end apart: 5, of which 2 were waited for; matrix products, arithmetic and copies ran while one was open for 44% of the time, Pallas kernels for 0%

commit v1 on v0

v1 whole, which is shorter than its diff:
```python
import functools

import jax
import jax.numpy as jnp
from jax import lax
from jax.experimental import pallas as pl
from jax.experimental.pallas import tpu as pltpu
from jax.sharding import PartitionSpec as P

MESH = pl.DeviceIdType.MESH
F32 = jnp.float32
BF16 = jnp.bfloat16
HIGHEST = lax.Precision.HIGHEST

ROWS = 256
HEADS = 8
WIDE = 512
STATE = 128
TAPS = 4
CUBE = 4

NN = (((1,), (0,)), ((), ()))
NT = (((1,), (1,)), ((), ()))
TN = (((0,), (0,)), ((), ()))


def dot(a, b, dims=NN):
    return lax.dot_general(a, b, dims, preferred_element_type=F32)


def exact_dot(a, b, dims=NN):
    return lax.dot_general(a, b, dims, precision=HIGHEST, preferred_element_type=F32)


def split(x):
    high = x.astype(BF16)
    return high, (x - high.astype(F32)).astype(BF16)


def wide_dot(x, y, dims=NN):
    high, low = split(x)
    return dot(high, y, dims) + dot(low, y, dims)


def scale_of(exponent):
    return jnp.exp2(exponent.astype(F32))


def exponent_of(largest):
    bits = jnp.floor(jnp.log(jnp.maximum(largest, 1e-36)) * 1.4426950408889634) + 1.0
    return jnp.clip(bits, -100.0, 100.0)


def code(x, exponent):
    return jnp.floor(x * scale_of(14.0 - exponent) + 0.5).astype(jnp.int32)


def pack(x):
    exponent = exponent_of(jnp.max(jnp.abs(x), axis=0, keepdims=True))
    return code(x, exponent).astype(jnp.int16), exponent


def pack_row(x):
    exponent = exponent_of(x)
    return code(x, exponent).astype(F32), exponent


def unpack(x, exponent):
    return x.astype(jnp.int32).astype(F32) * scale_of(exponent - 14.0)


def tile_of(*rows):
    row_of = lax.broadcasted_iota(jnp.int32, (16, 256), 0)
    tile = jnp.zeros((16, 256), F32)
    for i, row in enumerate(rows):
        tile = jnp.where(row_of == i, row, tile)
    return tile.astype(jnp.int32).astype(jnp.int16)


def kernel(
    chips,
    planes,
    tok_h,
    sta_h,
    log_h,
    bp_h,
    cp_h,
    gr_h,
    cw_h,
    cb_h,
    gain_h,
    in_h,
    sum_h,
    dec_h,
    o_in,
    o_sum,
    o_dec,
    tok,
    sta,
    log,
    bp,
    cp,
    gr,
    cw,
    cb,
    gain,
    ext,
    cnt,
    stk,
    act,
    slope,
    wact,
    wgr,
    win,
    wout,
    agr,
    sg,
    rowtot,
    xcol,
    loc,
    rx_full,
    rx_half,
    chip,
    l1,
    out2,
    l2,
    o3,
    full,
    rs_src,
    rs_dst,
    halo_s,
    halo_r,
    hb_s,
    hb_r,
    pg,
    pair_ss,
    pair_rs,
    halo_ss,
    halo_rs,
    l1_ss,
    l1_rs,
    l2_ss,
    l2_rs,
    l3_ss,
    l3_rs,
    fw_ss,
    fw_rs,
    sum_ss,
    sum_rs,
    ready,
    load,
    store,
):
    groups = chips // CUBE
    total = 2 * chips
    c = lax.axis_index("ctx")
    h = lax.axis_index("head")
    core = lax.rem(c, 2)
    other = 1 - core
    z = lax.div(c, 2)
    group = lax.div(z, CUBE)
    place = lax.rem(z, CUBE)
    after = (lax.rem(c + 1, total), h)
    before = (lax.rem(c + total - 1, total), h)
    partner = (2 * z + other, h)

    def in_cube(d):
        return lax.rem(place + d, CUBE)

    def cube_device(d):
        return (2 * (CUBE * group + in_cube(d)) + core, h)

    def other_group(d):
        return lax.rem(group + d, groups)

    def group_device(d):
        return (2 * (CUBE * other_group(d) + place) + core, h)

    def plane_head(d):
        return lax.rem(h + d, planes)

    barrier = pltpu.get_barrier_semaphore()
    peers = [after, before]
    peers += [cube_device(d) for d in range(1, CUBE)]
    nearby = sorted({1, groups - 1})
    peers += [group_device(d) for d in nearby]
    peers += [(c, plane_head(d)) for d in range(1, planes)]
    for peer in peers:
        pl.semaphore_signal(barrier, inc=1, device_id=peer, device_id_type=MESH)

    pairs = (
        (sta_h, sta),
        (log_h, log),
        (cp_h, cp),
        (gr_h, gr),
        (tok_h, tok),
        (cw_h, cw),
        (cb_h, cb),
        (bp_h, bp),
        (gain_h, gain),
    )
    loads = [
        pltpu.make_async_copy(src, dst, load.at[i]) for i, (src, dst) in enumerate(pairs)
    ]
    for copy in loads:
        copy.start()
    sends = []

    def send(src, dst, send_sem, recv_sem, device):
        copy = pltpu.make_async_remote_copy(
            src_ref=src,
            dst_ref=dst,
            send_sem=send_sem,
            recv_sem=recv_sem,
            device_id=device,
            device_id_type=MESH,
        )
        copy.start()
        sends.append(copy)
        return copy

    loads[0].wait()
    loads[1].wait()
    i0 = lax.broadcasted_iota(jnp.int32, (ROWS, ROWS), 0)
    i1 = lax.broadcasted_iota(jnp.int32, (ROWS, ROWS), 1)
    upper = (i0 <= i1).astype(F32)
    lower = (i0 >= i1).astype(F32)
    stk[0:HEADS] = log[...]
    stk[HEADS : 2 * HEADS] = jnp.broadcast_to(sta[...].astype(F32), (HEADS, ROWS))
    cum_row = exact_dot(stk[...], upper)
    cum_col = exact_dot(lower, stk[...], NT)
    cnt_row = cum_row[HEADS : HEADS + 1]
    cnt_col = cum_col[:, HEADS : HEADS + 1]
    cnt_last = cnt_col[ROWS - 1 : ROWS]
    log_col = cum_col[:, 0:HEADS]
    keep_in = (cnt_col == 0.0).astype(F32)
    keep_out = (cnt_col == cnt_last).astype(F32)
    cnt[0:8] = jnp.zeros((8, 128), F32)
    cnt[8 : 8 + ROWS] = jnp.broadcast_to(cnt_col, (ROWS, 128))
    cnt[8 + ROWS : 16 + ROWS] = jnp.broadcast_to(cnt_last, (8, 128))
    head_of = lax.broadcasted_iota(jnp.int32, (HEADS, WIDE), 0)
    lane_of = lax.broadcasted_iota(jnp.int32, (HEADS, WIDE), 1)
    pick = (lax.div(lane_of, WIDE // HEADS) == head_of).astype(F32)
    win[...] = exact_dot(jnp.exp(log_col) * keep_in, pick)
    wout[...] = exact_dot(jnp.exp(log_col[ROWS - 1 : ROWS] - log_col) * keep_out, pick)
    factor = win[ROWS - 1 : ROWS, :]
    for half in range(2):
        lanes = slice(256 * half, 256 * half + 256)
        for which in range(2):
            loc[which, half, STATE : STATE + 8] = jnp.broadcast_to(factor[:, lanes], (8, 256))

    loads[2].wait()
    loads[3].wait()
    for half in range(2):
        lanes = slice(256 * half, 256 * half + 256)
        high, low = split(win[:, lanes] * gr[:, lanes].astype(F32))
        wgr[0, :, lanes] = high
        wgr[1, :, lanes] = low
        loc[1, half, 0:STATE] = dot(cp[...], high, TN) + dot(cp[...], low, TN)

    for copy in loads[4:]:
        copy.wait()
    halo_s[...] = tok[ROWS - 16 :] * keep_out[ROWS - 16 :].astype(BF16)

    def convolve(first, rows):
        for chunk in range(4):
            lanes = slice(128 * chunk, 128 * chunk + 128)
            here = cnt[8 + first : 8 + first + rows]
            value = cb[:, lanes] + cw[0:1, lanes] * ext[8 + first : 8 + first + rows, lanes]
            for k in range(1, TAPS):
                rows_at = slice(8 - k + first, 8 - k + first + rows)
                valid = (here == cnt[rows_at]).astype(F32)
                value = value + cw[k : k + 1, lanes] * ext[rows_at, lanes] * valid
            sigma = 1.0 / (1.0 + jnp.exp(-value))
            act[first : first + rows, lanes] = (value * sigma).astype(BF16)
            slope[first : first + rows, lanes] = sigma * (1.0 + value * (1.0 - sigma))

    ext[0:8] = jnp.zeros((8, WIDE), F32)
    ext[8:] = tok[...].astype(F32)
    convolve(0, ROWS)

    def local_state(rows, half):
        lanes = slice(256 * half, 256 * half + 256)
        high, low = split(wout[rows, lanes] * act[rows, lanes].astype(F32))
        wact[0, rows, lanes] = high
        wact[1, rows, lanes] = low
        return dot(bp[rows], high, TN) + dot(bp[rows], low, TN)

    for half in range(2):
        loc[0, half, 0:STATE] = local_state(slice(16, ROWS), half)

    pl.semaphore_wait(barrier, len(peers))
    for d in nearby:
        pl.semaphore_signal(ready, inc=1, device_id=group_device(d), device_id_type=MESH)

    halo = send(halo_s, halo_r, halo_ss.at[0], halo_rs.at[0], after)
    halo.wait_recv()
    is_first = (c > 0).astype(F32)
    ext[0:8] = halo_r[8:16].astype(F32) * is_first
    convolve(0, 16)

    for half in range(2):
        loc[0, half, 0:STATE] += local_state(slice(0, 16), half)

    first = send(
        loc.at[core, other], rx_full.at[other], pair_ss.at[0], pair_rs.at[0], partner
    )
    second = send(loc.at[other, other], rx_half, pair_ss.at[1], pair_rs.at[1], partner)
    third = send(loc.at[core, core], rx_full.at[core], pair_ss.at[2], pair_rs.at[2], partner)
    first.wait_recv()
    second.wait_recv()
    f_own = loc[0, core, STATE : STATE + 1]
    f_other = rx_half[STATE : STATE + 1]
    is_late = core == 1
    factor_code, factor_exponent = pack_row(f_own * f_other)
    for s in range(CUBE):
        rows = slice(32 * s, 32 * s + 32)
        mine, e_mine = pack(rx_half[rows] + f_other * loc[core, core, rows])
        yours, e_yours = pack(loc[other, core, rows] + f_own * rx_full[core, rows])
        chip[s, pl.ds(pl.multiple_of(32 * core, 32), 32)] = mine
        chip[s, pl.ds(pl.multiple_of(32 * other, 32), 32)] = yours
        chip[s, 64:80] = tile_of(
            jnp.where(is_late, e_yours, e_mine),
            jnp.where(is_late, e_mine, e_yours),
            factor_exponent,
            factor_code,
        )

    l1[place] = chip[place]
    ups = []
    for d in range(1, CUBE):
        ups.append(
            send(chip.at[in_cube(d)], l1.at[place], l1_ss.at[d - 1], l1_rs.at[d - 1], cube_device(d))
        )

    gain_wide = exact_dot(jnp.broadcast_to(gain[...], (8, HEADS)), pick)[0:1]
    scores = dot(bp[...], cp[...], NT)
    bias = jnp.where((i0 <= i1) & (cnt_col == cnt_row), 0.0, -1e30)
    even = lax.broadcasted_iota(jnp.int32, (ROWS, 128), 1) < 64

    def intra(pair, begin):
        lanes = slice(128 * pair, 128 * pair + 128)
        parts = []
        for head in (2 * pair, 2 * pair + 1):
            decay = jnp.exp(cum_row[head : head + 1] - cum_col[:, head : head + 1] + bias)
            mixed = decay * scores
            parts.append(dot(mixed.astype(BF16), gr[:, lanes]))
            mine = even if head % 2 == 0 else ~even
            rows = jnp.where(mine, act[:, lanes].astype(F32), 0.0).astype(BF16)
            inner = dot(rows, gr[:, lanes], NT)
            if begin and head % 2 == 0:
                sg[...] = decay * inner
            else:
                sg[...] += decay * inner
            product = mixed * inner
            rowtot[head : head + 1] = jnp.sum(product, axis=0, keepdims=True)
            xcol[:, head : head + 1] = jnp.sum(product, axis=1, keepdims=True)
        agr[:, lanes] = jnp.where(even, parts[0], parts[1]) + gain_wide[:, lanes] * gr[
            :, lanes
        ].astype(F32)

    intra(0, True)
    intra(1, False)

    for copy in ups:
        copy.wait_recv()

    def unpack_slot(ref, j, arrays):
        tile = ref[j, 32 * arrays : 32 * arrays + 16].astype(jnp.int32).astype(F32)
        values = [
            unpack(ref[j, 32 * i : 32 * i + 32], tile[i : i + 1]) for i in range(arrays)
        ]
        factor = tile[arrays + 1 : arrays + 2] * scale_of(tile[arrays : arrays + 1] - 14.0)
        return values, factor

    slots = [unpack_slot(l1, j, 2) for j in range(CUBE)]

    def prefixes():
        values, factors = [jnp.zeros((32, 256), F32)], [jnp.ones((1, 256), F32)]
        for (state, _), f in slots:
            values.append(state + f * values[-1])
            factors.append(f * factors[-1])
        return values, factors

    def suffixes():
        values, factors = [jnp.zeros((32, 256), F32)], [jnp.ones((1, 256), F32)]
        for (_, adjoint), f in reversed(slots):
            values.append(adjoint + f * values[-1])
            factors.append(f * factors[-1])
        return values[::-1], factors[::-1]

    down, down_f = prefixes()
    up, up_f = suffixes()
    factor_code, factor_exponent = pack_row(down_f[CUBE])
    for kind, total_here in enumerate((down[CUBE], up[0])):
        coded, exponent = pack(total_here)
        out2[kind, 0:32] = coded
        out2[kind, 32:48] = tile_of(exponent, factor_exponent, factor_code)
    pl.semaphore_wait(ready, len(nearby))
    crosses = []
    for d in range(1, groups):
        kind = (other_group(d) < group).astype(jnp.int32)
        crosses.append(
            send(out2.at[kind], l2.at[group], l2_ss.at[d - 1], l2_rs.at[d - 1], group_device(d))
        )

    intra(2, False)
    intra(3, False)

    for copy in crosses:
        copy.wait_recv()
    totals = [unpack_slot(l2, u, 1) for u in range(groups)]
    from_before = jnp.zeros((32, 256), F32)
    for u in range(groups):
        (value,), f = totals[u]
        from_before = jnp.where(u < group, value + f * from_before, from_before)
    from_after = jnp.zeros((32, 256), F32)
    for u in reversed(range(groups)):
        (value,), f = totals[u]
        from_after = jnp.where(u > group, value + f * from_after, from_after)
    for j in range(CUBE):
        state, e_state = pack(down[j] + down_f[j] * from_before)
        adjoint, e_adjoint = pack(up[j + 1] + up_f[j + 1] * from_after)
        o3[j, 0:32] = state
        o3[j, 32:64] = adjoint
        o3[j, 64:80] = tile_of(e_state, e_adjoint)
    full[core, place] = o3[place]
    forwards = []
    backs = []
    for d in range(1, CUBE):
        backs.append(
            send(
                o3.at[in_cube(d)],
                full.at[core, place],
                l3_ss.at[d - 1],
                l3_rs.at[d - 1],
                cube_device(d),
            )
        )
    here = full.at[core, place]
    forwards.append(send(here, here, fw_ss.at[0], fw_rs.at[0], partner))

    high, low = split(sg[...])
    rs_src[:, 0:STATE] = dot(high, cp[...]) + dot(low, cp[...])
    rs_src[:, STATE:] = dot(high, bp[...], TN) + dot(low, bp[...], TN)

    for d in range(1, CUBE):
        backs[d - 1].wait_recv()
        slot = full.at[core, in_cube(CUBE - d)]
        forwards.append(send(slot, slot, fw_ss.at[d], fw_rs.at[d], partner))
    third.wait_recv()
    for copy in forwards:
        copy.wait_recv()

    late = (core == 1).astype(F32)
    early = 1.0 - late
    state_in, adjoint_in, end_row = [], [], []
    for half in range(2):
        f_other = rx_full[half, STATE : STATE + 1]
        received = rx_full[half, 0:STATE]
        f_own = loc[0, half, STATE : STATE + 1]
        tiles = full[half, :, 64:80].astype(jnp.int32).astype(F32)
        wide = unpack(full[half, :, 0:32], tiles[:, 0:1]).reshape(STATE, 256)
        state = late * received + (late * f_other + early) * wide
        wide = unpack(full[half, :, 32:64], tiles[:, 1:2]).reshape(STATE, 256)
        adjoint = early * received + (early * f_other + late) * wide
        state_out = loc[0, half, 0:STATE] + f_own * state
        end_row.append(jnp.sum(adjoint * state_out, axis=0, keepdims=True))
        state_in.append(state.astype(BF16))
        adjoint_in.append(adjoint.astype(BF16))

    b_part = rs_src[:, 0:STATE]
    c_part = rs_src[:, STATE:]
    for half in range(2):
        lanes = slice(256 * half, 256 * half + 256)
        for part in range(2):
            b_part = b_part + dot(wact[part, :, lanes], adjoint_in[half], NT)
            c_part = c_part + dot(wgr[part, :, lanes], state_in[half], NT)
    rs_src[:, 0:STATE] = b_part
    rs_src[:, STATE:] = c_part
    rs_dst[h] = rs_src[pl.ds(pl.multiple_of(16 * h, 16), 16)]
    sums = []
    for d in range(1, planes):
        rows = pl.ds(pl.multiple_of(16 * plane_head(d), 16), 16)
        sums.append(
            send(rs_src.at[rows], rs_dst.at[h], sum_ss.at[d - 1], sum_rs.at[d - 1], (c, plane_head(d)))
        )

    inter = jnp.zeros((HEADS, ROWS), F32)
    for half in range(2):
        lanes = slice(256 * half, 256 * half + 256)
        after_part = wout[:, lanes] * dot(bp[...], adjoint_in[half])
        before_part = win[:, lanes] * dot(cp[...], state_in[half])
        pg[0:ROWS, lanes] = (agr[:, lanes] + after_part) * slope[:, lanes]
        difference = before_part * gr[:, lanes].astype(F32) - after_part * act[:, lanes].astype(F32)
        inter = inter + exact_dot(pick[:, lanes], difference, NT)
    hb_s[...] = pg[0:8] * keep_in[0:8]
    back = send(hb_s, hb_r, halo_ss.at[1], halo_rs.at[1], before)

    ends = jnp.sum(pick * jnp.concatenate(end_row, axis=1), axis=1, keepdims=True)
    cum_total = rowtot[...] + inter - xcol[...].T[0:HEADS]
    o_dec[...] = exact_dot(cum_total, lower) + ends
    stores = [pltpu.make_async_copy(o_dec, dec_h, store.at[5])]
    stores[0].start()

    back.wait_recv()
    is_last = (c < total - 1).astype(F32)
    pg[ROWS:] = hb_r[...] * is_last
    for chunk in range(4):
        lanes = slice(128 * chunk, 128 * chunk + 128)
        value = cw[0:1, lanes] * pg[0:ROWS, lanes]
        for k in range(1, TAPS):
            valid = (cnt[8 + k : 8 + k + ROWS] == cnt[8 : 8 + ROWS]).astype(F32)
            value = value + cw[k : k + 1, lanes] * pg[k : k + ROWS, lanes] * valid
        o_in[:, lanes] = value
        stores.append(pltpu.make_async_copy(o_in.at[:, lanes], in_h.at[:, lanes], store.at[chunk]))
        stores[-1].start()

    for copy in sums:
        copy.wait_recv()
    result = rs_dst[0]
    for j in range(1, planes):
        result = result + rs_dst[j]
    o_sum[...] = result
    stores.append(pltpu.make_async_copy(o_sum, sum_h, store.at[4]))
    stores[-1].start()
    for copy in stores:
        copy.wait()

    for copy in sends:
        copy.wait_send()


def finish(a_in, a_sum, a_dec, o_in, o_b, o_c, o_dec, wide, sums, decay, load, store):
    def go(i, src, dst, sem):
        return pltpu.make_async_copy(src, dst, sem.at[i])

    quarter = ROWS // 4
    parts = [slice(quarter * i, quarter * i + quarter) for i in range(4)]
    pairs = [(a_in.at[p], wide.at[p], o_in.at[p]) for p in parts]
    loads = [go(i, src, mid, load) for i, (src, mid, _) in enumerate(pairs)]
    loads += [go(4, a_sum, sums, load), go(5, a_dec, decay, load)]
    stores = [go(i, mid, dst, store) for i, (_, mid, dst) in enumerate(pairs)]
    stores += [go(4, sums.at[:, 0:STATE], o_b, store), go(5, decay, o_dec, store)]
    stores += [go(6, sums.at[:, STATE : 2 * STATE], o_c, store)]
    for copy in loads:
        copy.start()
    for i in range(6):
        loads[i].wait()
        stores[i].start()
        if i == 4:
            stores[6].start()
    for copy in stores:
        copy.wait()


def body(tokens_in, starts, log_decay, b_proj, c_proj, out_grad, conv_weight, conv_bias, skip_gain):
    chips = lax.axis_size("ctx") // 2
    planes = lax.axis_size("head")
    groups = chips // CUBE
    own = ROWS // planes
    vmem = pltpu.VMEM
    dma = pltpu.SemaphoreType.DMA
    in_grad, sums, decay_grad = pl.pallas_call(
        functools.partial(kernel, chips, planes),
        out_shape=(
            jax.ShapeDtypeStruct((ROWS, WIDE), F32),
            jax.ShapeDtypeStruct((own, 2 * STATE), F32),
            jax.ShapeDtypeStruct((HEADS, ROWS), F32),
        ),
        in_specs=[pl.BlockSpec(memory_space=pltpu.HBM)] * 9,
        out_specs=[pl.BlockSpec(memory_space=pltpu.HBM)] * 3,
        scratch_shapes=[
            vmem((ROWS, WIDE), F32),
            vmem((own, 2 * STATE), F32),
            vmem((HEADS, ROWS), F32),
            vmem((ROWS, WIDE), BF16),
            vmem((1, ROWS), jnp.int32),
            vmem((HEADS, ROWS), F32),
            vmem((ROWS, STATE), BF16),
            vmem((ROWS, STATE), BF16),
            vmem((ROWS, WIDE), BF16),
            vmem((TAPS, WIDE), F32),
            vmem((1, WIDE), F32),
            vmem((1, HEADS), F32),
            vmem((8 + ROWS, WIDE), F32),
            vmem((16 + ROWS, 128), F32),
            vmem((2 * HEADS, ROWS), F32),
            vmem((ROWS, WIDE), BF16),
            vmem((ROWS, WIDE), F32),
            vmem((2, ROWS, WIDE), BF16),
            vmem((2, ROWS, WIDE), BF16),
            vmem((ROWS, WIDE), F32),
            vmem((ROWS, WIDE), F32),
            vmem((ROWS, WIDE), F32),
            vmem((ROWS, ROWS), F32),
            vmem((HEADS, ROWS), F32),
            vmem((ROWS, 128), F32),
            vmem((2, 2, STATE + 8, 256), F32),
            vmem((2, STATE + 8, 256), F32),
            vmem((STATE + 8, 256), F32),
            vmem((CUBE, 80, 256), jnp.int16),
            vmem((CUBE, 80, 256), jnp.int16),
            vmem((2, 48, 256), jnp.int16),
            vmem((groups, 48, 256), jnp.int16),
            vmem((CUBE, 80, 256), jnp.int16),
            vmem((2, CUBE, 80, 256), jnp.int16),
            vmem((ROWS, 2 * STATE), F32),
            vmem((planes, own, 2 * STATE), F32),
            vmem((16, WIDE), BF16),
            vmem((16, WIDE), BF16),
            vmem((8, WIDE), F32),
            vmem((8, WIDE), F32),
            vmem((8 + ROWS, WIDE), F32),
            dma((3,)),
            dma((3,)),
            dma((2,)),
            dma((2,)),
            dma((CUBE - 1,)),
            dma((CUBE - 1,)),
            dma((groups - 1,)),
            dma((groups - 1,)),
            dma((CUBE - 1,)),
            dma((CUBE - 1,)),
            dma((CUBE,)),
            dma((CUBE,)),
            dma((max(planes - 1, 1),)),
            dma((max(planes - 1, 1),)),
            pltpu.SemaphoreType.REGULAR,
            dma((9,)),
            dma((6,)),
        ],
        compiler_params=pltpu.CompilerParams(
            collective_id=0, has_side_effects=True, vmem_limit_bytes=63 * 1024 * 1024
        ),
        name="layer",
    )(
        tokens_in,
        starts.reshape(1, ROWS),
        log_decay,
        b_proj,
        c_proj,
        out_grad,
        conv_weight,
        conv_bias.reshape(1, WIDE),
        skip_gain.reshape(1, HEADS),
    )
    in_grad, b_grad, c_grad, decay_grad = pl.pallas_call(
        finish,
        out_shape=(
            jax.ShapeDtypeStruct((ROWS, WIDE), F32),
            jax.ShapeDtypeStruct((own, STATE), F32),
            jax.ShapeDtypeStruct((own, STATE), F32),
            jax.ShapeDtypeStruct((HEADS, ROWS), F32),
        ),
        in_specs=[pl.BlockSpec(memory_space=pl.ANY)] * 3,
        out_specs=[pl.BlockSpec(memory_space=pltpu.HBM)] * 4,
        scratch_shapes=[
            vmem((ROWS, WIDE), F32),
            vmem((own, 2 * STATE), F32),
            vmem((HEADS, ROWS), F32),
            dma((6,)),
            dma((7,)),
        ],
        compiler_params=pltpu.CompilerParams(vmem_limit_bytes=63 * 1024 * 1024),
        name="finish",
    )(in_grad, sums, decay_grad)
    return (in_grad, b_grad, c_grad, decay_grad)


def solution(mesh):
    placed = (
        P("ctx", "head"),
        P("ctx"),
        P("head", "ctx"),
        P("ctx", None),
        P("ctx", None),
        P("ctx", "head"),
        P(None, "head"),
        P("head"),
        P("head"),
    )
    return jax.shard_map(
        body,
        mesh=mesh,
        in_specs=placed,
        out_specs=(
            P("ctx", "head"),
            P(("ctx", "head"), None),
            P(("ctx", "head"), None),
            P("head", "ctx"),
        ),
        check_vma=False,
    )
```

time: 354 us -> 49.6 us (0.14); the launches traced: 350 us -> 49.5 us
  local copies, waits for them, and re-layouts: 119 us -> 0 us
  waiting for transfers between devices: 108 us -> 0 us
  blocking collectives: 52.1 us -> 0 us
  Pallas kernels: 0 us -> 48.8 us
  other arithmetic: 25.7 us -> 0 us
  matrix products: 18.6 us -> 0 us
  between operations: 14.9 us -> 0.64 us
  starting transfers between devices: 9.16 us -> 0 us
    unnamed x4 -> x0, waiting for transfers between devices: 79.7 us -> none
    dynamic_slice x136 -> x0, local copies, waits for them, and re-layouts: 75.2 us -> none  [the longest x64 37.7 us: backward_step(): gathered_adjoint[source] + gathered_factor[source][:, None, None] * adjoint]
    unnamed x1 -> x0, blocking collectives: 52.1 us -> none
    pallas_call x0 -> x2, Pallas kernels: none -> 48.8 us  [the longest x1 47 us: body(): pl.pallas_call(functools.partial(kernel, chips, planes), out_shape=(jax.S...]
    all_gather x2 -> x0, waiting for transfers between devices: 28.2 us -> none  [the longest x1 28.1 us: body(): lax.all_gather(state_local[None], 'ctx', axis=0, tiled=True)]
    mul x64 -> x0, local copies, waits for them, and re-layouts: 22.5 us -> none  [the longest x32 22.1 us: forward_step(): gathered_factor[counter][:, None, None] * state]
    dot_general x25 -> x0, matrix products: 18.6 us -> none  [the longest x8 7.89 us: one_head(): lax.dot_general(mixed, grad_wide, (((0,), (0,)), ((), ())), precision=hig...]
    dynamic_update_slice x8 -> x0, local copies, waits for them, and re-layouts: 10.5 us -> none  [intra_heads(): lax.scan(one_head, jnp.zeros_like(scores), (act_heads, grad_heads, cum_de...]
  transfers between devices with their start and end apart: 5 -> 0, of which waited for: 2 -> 0; matrix products, arithmetic and copies ran while one was open for 44% -> 0% of each run, Pallas kernels for 0% -> 0%
where the time goes in v1:
time: 49.6 us; the launch traced here: 49.5 us
  Pallas kernels  48.8 us (98%)
  between operations  0.64 us (1%)
    pallas_call x1, Pallas kernels, body(): pl.pallas_call(functools.partial(kernel, chips, planes), out_shape=(jax.S...  47 us
    pallas_call x1, Pallas kernels, body(): pl.pallas_call(finish, out_shape=(jax.ShapeDtypeStruct((ROWS, WIDE), F32)...  1.87 us

profile of v1, /device:TPU:1, one launch (start us, length us, event | category | flops | bytes accessed | tf_op | source)
XLA Modules:
  0.0 49.5 jit_solution(17035020663190303689)
XLA Ops:
  0.6 47.0 %layer.1 = (f32[256,512]{1,0:T(8,128)}, f32[16,256]{1,0:T(8,128)}, f32[8,256]{1,0:T(8,128)}) custom-call(bf16[256,512]{1,0:T(8,128)(2,1)} %tok_h.1, s32[1,256]{1,0:T(1,128)} %bitcast.4, f32[8,256]{1,0:T(8,128)} %log_h.1, bf16[256,128]{1,0:T(8,128)(2,1)} %bp_h.1, bf16[256,128]{1,0:T(8,128)(2,1)} %cp_h.1, bf16[256,512]{1,0:T(8,128)(2,1)} %gr_h.1, ...), custom_call_target="tpu_custom_call" | custom-call | tf_op jit(solution)/shard_map/layer/pallas_call | solution.py:564
  47.6 1.9 %finish.1 = (f32[256,512]{1,0:T(8,128)}, f32[16,128]{1,0:T(8,128)}, f32[16,128]{1,0:T(8,128)}, f32[8,256]{1,0:T(8,128)}) custom-call(f32[256,512]{1,0:T(8,128)} %get-tuple-element.7.a_in, f32[16,256]{1,0:T(8,128)} %get-tuple-element.8.a_sum, f32[8,256]{1,0:T(8,128)} %get-tuple-element.9.a_dec), custom_call_target="tpu_custom_call" | custom-call | tf_op jit(solution)/shard_map/finish/pallas_call | solution.py:648

commit v2 on v1

--- a/solution.py
+++ b/solution.py
@@ -70,11 +70,16 @@
 
 
 def tile_of(*rows):
-    row_of = lax.broadcasted_iota(jnp.int32, (16, 256), 0)
-    tile = jnp.zeros((16, 256), F32)
+    row_of = lax.broadcasted_iota(jnp.int32, (16, 128), 0)
+    tile = jnp.zeros((16, 128), F32)
     for i, row in enumerate(rows):
         tile = jnp.where(row_of == i, row, tile)
     return tile.astype(jnp.int32).astype(jnp.int16)
+
+
+def block_of(place):
+    row, lane = 64 * (place // 2), 128 * (place % 2)
+    return slice(row, row + 64), slice(lane, lane + 128)
 
 
 def kernel(
@@ -93,7 +98,6 @@
     sum_h,
     dec_h,
     o_in,
-    o_sum,
     o_dec,
     tok,
     sta,
@@ -127,7 +131,7 @@
     o3,
     full,
     rs_src,
-    rs_dst,
+    rs_out,
     halo_s,
     halo_r,
     hb_s,
@@ -314,16 +318,18 @@
     is_late = core == 1
     factor_code, factor_exponent = pack_row(f_own * f_other)
     for s in range(CUBE):
-        rows = slice(32 * s, 32 * s + 32)
-        mine, e_mine = pack(rx_half[rows] + f_other * loc[core, core, rows])
-        yours, e_yours = pack(loc[other, core, rows] + f_own * rx_full[core, rows])
-        chip[s, pl.ds(pl.multiple_of(32 * core, 32), 32)] = mine
-        chip[s, pl.ds(pl.multiple_of(32 * other, 32), 32)] = yours
-        chip[s, 64:80] = tile_of(
+        rows, lanes = block_of(s)
+        mine, e_mine = pack(rx_half[rows, lanes] + f_other[:, lanes] * loc[core, core, rows, lanes])
+        yours, e_yours = pack(
+            loc[other, core, rows, lanes] + f_own[:, lanes] * rx_full[core, rows, lanes]
+        )
+        chip[s, pl.ds(pl.multiple_of(64 * core, 64), 64)] = mine
+        chip[s, pl.ds(pl.multiple_of(64 * other, 64), 64)] = yours
+        chip[s, 128:144] = tile_of(
             jnp.where(is_late, e_yours, e_mine),
             jnp.where(is_late, e_mine, e_yours),
-            factor_exponent,
-            factor_code,
+            factor_exponent[:, lanes],
+            factor_code[:, lanes],
         )
 
     l1[place] = chip[place]
@@ -366,9 +372,9 @@
         copy.wait_recv()
 
     def unpack_slot(ref, j, arrays):
-        tile = ref[j, 32 * arrays : 32 * arrays + 16].astype(jnp.int32).astype(F32)
+        tile = ref[j, 64 * arrays : 64 * arrays + 16].astype(jnp.int32).astype(F32)
         values = [
-            unpack(ref[j, 32 * i : 32 * i + 32], tile[i : i + 1]) for i in range(arrays)
+            unpack(ref[j, 64 * i : 64 * i + 64], tile[i : i + 1]) for i in range(arrays)
         ]
         factor = tile[arrays + 1 : arrays + 2] * scale_of(tile[arrays : arrays + 1] - 14.0)
         return values, factor
@@ -376,14 +382,14 @@
     slots = [unpack_slot(l1, j, 2) for j in range(CUBE)]
 
     def prefixes():
-        values, factors = [jnp.zeros((32, 256), F32)], [jnp.ones((1, 256), F32)]
+        values, factors = [jnp.zeros((64, 128), F32)], [jnp.ones((1, 128), F32)]
         for (state, _), f in slots:
             values.append(state + f * values[-1])
             factors.append(f * factors[-1])
         return values, factors
 
     def suffixes():
-        values, factors = [jnp.zeros((32, 256), F32)], [jnp.ones((1, 256), F32)]
+        values, factors = [jnp.zeros((64, 128), F32)], [jnp.ones((1, 128), F32)]
         for (_, adjoint), f in reversed(slots):
             values.append(adjoint + f * values[-1])
             factors.append(f * factors[-1])
@@ -394,8 +400,8 @@
     factor_code, factor_exponent = pack_row(down_f[CUBE])
     for kind, total_here in enumerate((down[CUBE], up[0])):
         coded, exponent = pack(total_here)
-        out2[kind, 0:32] = coded
-        out2[kind, 32:48] = tile_of(exponent, factor_exponent, factor_code)
+        out2[kind, 0:64] = coded
+        out2[kind, 64:80] = tile_of(exponent, factor_exponent, factor_code)
     pl.semaphore_wait(ready, len(nearby))
     crosses = []
     for d in range(1, groups):
@@ -410,20 +416,20 @@
     for copy in crosses:
         copy.wait_recv()
     totals = [unpack_slot(l2, u, 1) for u in range(groups)]
-    from_before = jnp.zeros((32, 256), F32)
+    from_before = jnp.zeros((64, 128), F32)
     for u in range(groups):
         (value,), f = totals[u]
         from_before = jnp.where(u < group, value + f * from_before, from_before)
-    from_after = jnp.zeros((32, 256), F32)
+    from_after = jnp.zeros((64, 128), F32)
     for u in reversed(range(groups)):
         (value,), f = totals[u]
         from_after = jnp.where(u > group, value + f * from_after, from_after)
     for j in range(CUBE):
         state, e_state = pack(down[j] + down_f[j] * from_before)
         adjoint, e_adjoint = pack(up[j + 1] + up_f[j + 1] * from_after)
-        o3[j, 0:32] = state
-        o3[j, 32:64] = adjoint
-        o3[j, 64:80] = tile_of(e_state, e_adjoint)
+        o3[j, 0:64] = state
+        o3[j, 64:128] = adjoint
+        o3[j, 128:144] = tile_of(e_state, e_adjoint)
     full[core, place] = o3[place]
     forwards = []
     backs = []
@@ -452,6 +458,16 @@
     for copy in forwards:
         copy.wait_recv()
 
+    def incoming(half, which):
+        blocks = []
+        for s in range(CUBE):
+            tile = full[half, s, 128:144].astype(jnp.int32).astype(F32)
+            blocks.append(
+                unpack(full[half, s, 64 * which : 64 * which + 64], tile[which : which + 1])
+            )
+        top = jnp.concatenate(blocks[0:2], axis=1)
+        return jnp.concatenate([top, jnp.concatenate(blocks[2:4], axis=1)], axis=0)
+
     late = (core == 1).astype(F32)
     early = 1.0 - late
     state_in, adjoint_in, end_row = [], [], []
@@ -459,38 +475,40 @@
         f_other = rx_full[half, STATE : STATE + 1]
         received = rx_full[half, 0:STATE]
         f_own = loc[0, half, STATE : STATE + 1]
-        tiles = full[half, :, 64:80].astype(jnp.int32).astype(F32)
-        wide = unpack(full[half, :, 0:32], tiles[:, 0:1]).reshape(STATE, 256)
+        wide = incoming(half, 0)
         state = late * received + (late * f_other + early) * wide
-        wide = unpack(full[half, :, 32:64], tiles[:, 1:2]).reshape(STATE, 256)
+        wide = incoming(half, 1)
         adjoint = early * received + (early * f_other + late) * wide
         state_out = loc[0, half, 0:STATE] + f_own * state
         end_row.append(jnp.sum(adjoint * state_out, axis=0, keepdims=True))
-        state_in.append(state.astype(BF16))
-        adjoint_in.append(adjoint.astype(BF16))
+        state_in.append(split(state))
+        adjoint_in.append(split(adjoint))
 
     b_part = rs_src[:, 0:STATE]
     c_part = rs_src[:, STATE:]
     for half in range(2):
         lanes = slice(256 * half, 256 * half + 256)
-        for part in range(2):
-            b_part = b_part + dot(wact[part, :, lanes], adjoint_in[half], NT)
-            c_part = c_part + dot(wgr[part, :, lanes], state_in[half], NT)
-    rs_src[:, 0:STATE] = b_part
-    rs_src[:, STATE:] = c_part
-    rs_dst[h] = rs_src[pl.ds(pl.multiple_of(16 * h, 16), 16)]
+        for left, right in ((0, 0), (1, 0), (0, 1)):
+            b_part = b_part + dot(wact[left, :, lanes], adjoint_in[half][right], NT)
+            c_part = c_part + dot(wgr[left, :, lanes], state_in[half][right], NT)
+    rs_out[:, 0:STATE] = b_part.astype(BF16)
+    rs_out[:, STATE:] = c_part.astype(BF16)
+    keep = pltpu.make_async_copy(
+        rs_out.at[pl.ds(pl.multiple_of(16 * h, 16), 16)], sum_h.at[h], store.at[4]
+    )
+    keep.start()
     sums = []
     for d in range(1, planes):
         rows = pl.ds(pl.multiple_of(16 * plane_head(d), 16), 16)
         sums.append(
-            send(rs_src.at[rows], rs_dst.at[h], sum_ss.at[d - 1], sum_rs.at[d - 1], (c, plane_head(d)))
+            send(rs_out.at[rows], sum_h.at[h], sum_ss.at[d - 1], sum_rs.at[d - 1], (c, plane_head(d)))
         )
 
     inter = jnp.zeros((HEADS, ROWS), F32)
     for half in range(2):
         lanes = slice(256 * half, 256 * half + 256)
-        after_part = wout[:, lanes] * dot(bp[...], adjoint_in[half])
-        before_part = win[:, lanes] * dot(cp[...], state_in[half])
+        after_part = wout[:, lanes] * dot(bp[...], adjoint_in[half][0])
+        before_part = win[:, lanes] * dot(cp[...], state_in[half][0])
         pg[0:ROWS, lanes] = (agr[:, lanes] + after_part) * slope[:, lanes]
         difference = before_part * gr[:, lanes].astype(F32) - after_part * act[:, lanes].astype(F32)
         inter = inter + exact_dot(pick[:, lanes], difference, NT)
@@ -518,12 +536,7 @@
 
     for copy in sums:
         copy.wait_recv()
-    result = rs_dst[0]
-    for j in range(1, planes):
-        result = result + rs_dst[j]
-    o_sum[...] = result
-    stores.append(pltpu.make_async_copy(o_sum, sum_h, store.at[4]))
-    stores[-1].start()
+    stores.append(keep)
     for copy in stores:
         copy.wait()
 
@@ -531,25 +544,31 @@
         copy.wait_send()
 
 
-def finish(a_in, a_sum, a_dec, o_in, o_b, o_c, o_dec, wide, sums, decay, load, store):
+def finish(a_in, a_sum, a_dec, o_in, o_b, o_c, o_dec, wide, sums, both, decay, load, store):
     def go(i, src, dst, sem):
         return pltpu.make_async_copy(src, dst, sem.at[i])
 
-    quarter = ROWS // 4
-    parts = [slice(quarter * i, quarter * i + quarter) for i in range(4)]
-    pairs = [(a_in.at[p], wide.at[p], o_in.at[p]) for p in parts]
-    loads = [go(i, src, mid, load) for i, (src, mid, _) in enumerate(pairs)]
-    loads += [go(4, a_sum, sums, load), go(5, a_dec, decay, load)]
-    stores = [go(i, mid, dst, store) for i, (_, mid, dst) in enumerate(pairs)]
-    stores += [go(4, sums.at[:, 0:STATE], o_b, store), go(5, decay, o_dec, store)]
-    stores += [go(6, sums.at[:, STATE : 2 * STATE], o_c, store)]
+    half = ROWS // 2
+    triples = [(a_sum, sums, None)]
+    triples += [(a_in.at[p], wide.at[p], o_in.at[p]) for p in (pl.ds(0, half), pl.ds(half, half))]
+    triples += [(a_dec, decay, o_dec)]
+    loads = [go(i, src, mid, load) for i, (src, mid, _) in enumerate(triples)]
+    stores = [go(0, both.at[0], o_b, store)]
+    stores += [go(i, mid, dst, store) for i, (_, mid, dst) in enumerate(triples) if i > 0]
+    stores += [go(4, both.at[1], o_c, store)]
     for copy in loads:
         copy.start()
-    for i in range(6):
+    for i in range(1, 4):
         loads[i].wait()
         stores[i].start()
-        if i == 4:
-            stores[6].start()
+    loads[0].wait()
+    total = sums[0].astype(F32)
+    for j in range(1, sums.shape[0]):
+        total = total + sums[j].astype(F32)
+    both[0] = total[:, 0:STATE]
+    both[1] = total[:, STATE:]
+    stores[0].start()
+    stores[4].start()
     for copy in stores:
         copy.wait()
 
@@ -565,14 +584,13 @@
         functools.partial(kernel, chips, planes),
         out_shape=(
             jax.ShapeDtypeStruct((ROWS, WIDE), F32),
-            jax.ShapeDtypeStruct((own, 2 * STATE), F32),
+            jax.ShapeDtypeStruct((planes, own, 2 * STATE), BF16),
             jax.ShapeDtypeStruct((HEADS, ROWS), F32),
         ),
         in_specs=[pl.BlockSpec(memory_space=pltpu.HBM)] * 9,
         out_specs=[pl.BlockSpec(memory_space=pltpu.HBM)] * 3,
         scratch_shapes=[
             vmem((ROWS, WIDE), F32),
-            vmem((own, 2 * STATE), F32),
             vmem((HEADS, ROWS), F32),
             vmem((ROWS, WIDE), BF16),
             vmem((1, ROWS), jnp.int32),
@@ -599,14 +617,14 @@
             vmem((2, 2, STATE + 8, 256), F32),
             vmem((2, STATE + 8, 256), F32),
             vmem((STATE + 8, 256), F32),
-            vmem((CUBE, 80, 256), jnp.int16),
-            vmem((CUBE, 80, 256), jnp.int16),
-            vmem((2, 48, 256), jnp.int16),
-            vmem((groups, 48, 256), jnp.int16),
-            vmem((CUBE, 80, 256), jnp.int16),
-            vmem((2, CUBE, 80, 256), jnp.int16),
+            vmem((CUBE, 144, 128), jnp.int16),
+            vmem((CUBE, 144, 128), jnp.int16),
+            vmem((2, 80, 128), jnp.int16),
+            vmem((groups, 80, 128), jnp.int16),
+            vmem((CUBE, 144, 128), jnp.int16),
+            vmem((2, CUBE, 144, 128), jnp.int16),
             vmem((ROWS, 2 * STATE), F32),
-            vmem((planes, own, 2 * STATE), F32),
+            vmem((ROWS, 2 * STATE), BF16),
             vmem((16, WIDE), BF16),
             vmem((16, WIDE), BF16),
             vmem((8, WIDE), F32),
@@ -657,10 +675,11 @@
         out_specs=[pl.BlockSpec(memory_space=pltpu.HBM)] * 4,
         scratch_shapes=[
             vmem((ROWS, WIDE), F32),
-            vmem((own, 2 * STATE), F32),
+            vmem((planes, own, 2 * STATE), BF16),
+            vmem((2, own, STATE), F32),
             vmem((HEADS, ROWS), F32),
-            dma((6,)),
-            dma((7,)),
+            dma((4,)),
+            dma((5,)),
         ],
         compiler_params=pltpu.CompilerParams(vmem_limit_bytes=63 * 1024 * 1024),
         name="finish",

time: 49.6 us -> 47.8 us (0.964)
  Pallas kernels: 48.8 us -> 47 us
    pallas_call x1, Pallas kernels: 47 us -> 45.1 us  [body(): pl.pallas_call(functools.partial(kernel, chips, planes), out_shape=(jax.S...]
where the time goes in v2:
time: 47.8 us; the launch traced here: 47.6 us
  Pallas kernels  47 us (98%)
  between operations  0.64 us (1%)
    pallas_call x1, Pallas kernels, body(): pl.pallas_call(functools.partial(kernel, chips, planes), out_shape=(jax.S...  45.1 us
    pallas_call x1, Pallas kernels, body(): pl.pallas_call(finish, out_shape=(jax.ShapeDtypeStruct((ROWS, WIDE), F32)...  1.89 us

profile of v2, /device:TPU:1, one launch (start us, length us, event | category | flops | bytes accessed | tf_op | source)
XLA Modules:
  0.0 47.6 jit_solution(18118608117621550383)
XLA Ops:
  0.6 45.1 %layer.1 = (f32[256,512]{1,0:T(8,128)}, bf16[16,16,256]{2,1,0:T(8,128)(2,1)}, f32[8,256]{1,0:T(8,128)}) custom-call(bf16[256,512]{1,0:T(8,128)(2,1)} %tok_h.1, s32[1,256]{1,0:T(1,128)} %bitcast.4, f32[8,256]{1,0:T(8,128)} %log_h.1, bf16[256,128]{1,0:T(8,128)(2,1)} %bp_h.1, bf16[256,128]{1,0:T(8,128)(2,1)} %cp_h.1, bf16[256,512]{1,0:T(8,128)(2,1)} %gr_h.1, ...), custom_call_target="tpu_custom_call" | custom-call | tf_op jit(solution)/shard_map/layer/pallas_call | solution.py:583
  45.7 1.9 %finish.1 = (f32[256,512]{1,0:T(8,128)}, f32[16,128]{1,0:T(8,128)}, f32[16,128]{1,0:T(8,128)}, f32[8,256]{1,0:T(8,128)}) custom-call(f32[256,512]{1,0:T(8,128)} %get-tuple-element.7.a_in, bf16[16,16,256]{2,1,0:T(8,128)(2,1)} %get-tuple-element.8.a_sum, f32[8,256]{1,0:T(8,128)} %get-tuple-element.9.a_dec), custom_call_target="tpu_custom_call" | custom-call | tf_op jit(solution)/shard_map/finish/pallas_call | solution.py:666

commit v3 on v2

--- a/solution.py
+++ b/solution.py
@@ -1,4 +1,5 @@
 import functools
+import math
 
 import jax
 import jax.numpy as jnp
@@ -35,6 +36,15 @@
 def split(x):
     high = x.astype(BF16)
     return high, (x - high.astype(F32)).astype(BF16)
+
+
+def sum_dot(x, ones, dims=NN, first=True):
+    high = x.astype(BF16)
+    rest = x - high.astype(F32)
+    middle = rest.astype(BF16)
+    low = (rest - middle.astype(F32)).astype(BF16)
+    parts = [dot(p, ones, dims) if first else dot(ones, p, dims) for p in (high, middle, low)]
+    return parts[0] + (parts[1] + parts[2])
 
 
 def wide_dot(x, y, dims=NN):
@@ -151,11 +161,15 @@
     fw_rs,
     sum_ss,
     sum_rs,
-    ready,
+    row_ready,
+    edge_ready,
+    cube_ready,
+    far_ready,
     load,
     store,
 ):
     groups = chips // CUBE
+    side = math.isqrt(planes)
     total = 2 * chips
     c = lax.axis_index("ctx")
     h = lax.axis_index("head")
@@ -180,15 +194,27 @@
     def group_device(d):
         return (2 * (CUBE * other_group(d) + place) + core, h)
 
-    def plane_head(d):
-        return lax.rem(h + d, planes)
+    def along(d):
+        return lax.div(h, side) * side + lax.rem(lax.rem(h, side) + d, side)
+
+    def across(d):
+        return lax.rem(h + side * d, planes)
+
+    steps = [(dx, dy) for dx in range(side) for dy in range(side) if dx + dy > 0]
+    steps.sort(key=lambda step: -sum(min(d, side - d) for d in step))
+
+    def plane_head(step):
+        row = lax.rem(lax.div(h, side) + step[0], side)
+        return side * row + lax.rem(lax.rem(h, side) + step[1], side)
+
+    def chip_device(d):
+        return (2 * lax.rem(z + d + chips, chips) + core, h)
 
     barrier = pltpu.get_barrier_semaphore()
-    peers = [after, before]
+    peers = [after, before, chip_device(1), chip_device(-1)]
     peers += [cube_device(d) for d in range(1, CUBE)]
-    nearby = sorted({1, groups - 1})
-    peers += [group_device(d) for d in nearby]
-    peers += [(c, plane_head(d)) for d in range(1, planes)]
+    peers += [(c, along(d)) for d in range(1, side)]
+    peers += [(c, across(d)) for d in range(1, side)]
     for peer in peers:
         pl.semaphore_signal(barrier, inc=1, device_id=peer, device_id_type=MESH)
 
@@ -231,8 +257,8 @@
     lower = (i0 >= i1).astype(F32)
     stk[0:HEADS] = log[...]
     stk[HEADS : 2 * HEADS] = jnp.broadcast_to(sta[...].astype(F32), (HEADS, ROWS))
-    cum_row = exact_dot(stk[...], upper)
-    cum_col = exact_dot(lower, stk[...], NT)
+    cum_row = sum_dot(stk[...], upper.astype(BF16))
+    cum_col = sum_dot(stk[...], lower.astype(BF16), NT, first=False)
     cnt_row = cum_row[HEADS : HEADS + 1]
     cnt_col = cum_col[:, HEADS : HEADS + 1]
     cnt_last = cnt_col[ROWS - 1 : ROWS]
@@ -245,8 +271,9 @@
     head_of = lax.broadcasted_iota(jnp.int32, (HEADS, WIDE), 0)
     lane_of = lax.broadcasted_iota(jnp.int32, (HEADS, WIDE), 1)
     pick = (lax.div(lane_of, WIDE // HEADS) == head_of).astype(F32)
-    win[...] = exact_dot(jnp.exp(log_col) * keep_in, pick)
-    wout[...] = exact_dot(jnp.exp(log_col[ROWS - 1 : ROWS] - log_col) * keep_out, pick)
+    picked = pick.astype(BF16)
+    win[...] = wide_dot(jnp.exp(log_col) * keep_in, picked)
+    wout[...] = wide_dot(jnp.exp(log_col[ROWS - 1 : ROWS] - log_col) * keep_out, picked)
     factor = win[ROWS - 1 : ROWS, :]
     for half in range(2):
         lanes = slice(256 * half, 256 * half + 256)
@@ -294,10 +321,16 @@
         loc[0, half, 0:STATE] = local_state(slice(16, ROWS), half)
 
     pl.semaphore_wait(barrier, len(peers))
-    for d in nearby:
-        pl.semaphore_signal(ready, inc=1, device_id=group_device(d), device_id_type=MESH)
-
     halo = send(halo_s, halo_r, halo_ss.at[0], halo_rs.at[0], after)
+    lowest, highest = place == 0, place == CUBE - 1
+    for d in range(1, side):
+        pl.semaphore_signal(row_ready, inc=1, device_id=(c, across(d)), device_id_type=MESH)
+    for edge, d in ((lowest, -1), (highest, 1)):
+
+        @pl.when(edge)
+        def _():
+            pl.semaphore_signal(edge_ready, inc=1, device_id=chip_device(d), device_id_type=MESH)
+
     halo.wait_recv()
     is_first = (c > 0).astype(F32)
     ext[0:8] = halo_r[8:16].astype(F32) * is_first
@@ -311,6 +344,15 @@
     )
     second = send(loc.at[other, other], rx_half, pair_ss.at[1], pair_rs.at[1], partner)
     third = send(loc.at[core, core], rx_full.at[core], pair_ss.at[2], pair_rs.at[2], partner)
+
+    @pl.when(lowest | highest)
+    def _():
+        pl.semaphore_wait(edge_ready, 1)
+        for d in range(1, CUBE):
+            pl.semaphore_signal(
+                cube_ready, inc=1, device_id=cube_device(d), device_id_type=MESH
+            )
+
     first.wait_recv()
     second.wait_recv()
     f_own = loc[0, core, STATE : STATE + 1]
@@ -339,6 +381,15 @@
             send(chip.at[in_cube(d)], l1.at[place], l1_ss.at[d - 1], l1_rs.at[d - 1], cube_device(d))
         )
 
+    inside = jnp.logical_not(lowest | highest)
+    middle = (group > 0) & (group < groups - 1)
+    upper_half = group >= 2
+    pl.semaphore_wait(cube_ready, 1 + inside.astype(jnp.int32))
+
+    @pl.when(middle)
+    def _():
+        pl.semaphore_signal(far_ready, inc=1, device_id=group_device(1), device_id_type=MESH)
+
     gain_wide = exact_dot(jnp.broadcast_to(gain[...], (8, HEADS)), pick)[0:1]
     scores = dot(bp[...], cp[...], NT)
     bias = jnp.where((i0 <= i1) & (cnt_col == cnt_row), 0.0, -1e30)
@@ -402,19 +453,42 @@
         coded, exponent = pack(total_here)
         out2[kind, 0:64] = coded
         out2[kind, 64:80] = tile_of(exponent, factor_exponent, factor_code)
-    pl.semaphore_wait(ready, len(nearby))
     crosses = []
-    for d in range(1, groups):
+    for i, d in enumerate((1, groups - 1)):
         kind = (other_group(d) < group).astype(jnp.int32)
         crosses.append(
-            send(out2.at[kind], l2.at[group], l2_ss.at[d - 1], l2_rs.at[d - 1], group_device(d))
+            send(out2.at[kind], l2.at[group], l2_ss.at[i], l2_rs.at[i], group_device(d))
         )
+
+    def to_group(src, slot, i, d):
+        return pltpu.make_async_remote_copy(
+            src_ref=src,
+            dst_ref=l2.at[slot],
+            send_sem=l2_ss.at[i],
+            recv_sem=l2_rs.at[2],
+            device_id=group_device(d),
+            device_id_type=MESH,
+        )
+
+    relay = to_group(l2.at[other_group(groups - 1)], other_group(groups - 1), 2, 1)
+    direct = to_group(out2.at[1], group, 3, 2)
+
+    @pl.when(upper_half)
+    def _():
+        pl.semaphore_wait(far_ready, 1)
+        direct.start()
 
     intra(2, False)
     intra(3, False)
 
-    for copy in crosses:
-        copy.wait_recv()
+    crosses[0].wait_recv()
+
+    @pl.when(middle)
+    def _():
+        relay.start()
+
+    crosses[1].wait_recv()
+    relay.wait_recv()
     totals = [unpack_slot(l2, u, 1) for u in range(groups)]
     from_before = jnp.zeros((64, 128), F32)
     for u in range(groups):
@@ -497,11 +571,13 @@
         rs_out.at[pl.ds(pl.multiple_of(16 * h, 16), 16)], sum_h.at[h], store.at[4]
     )
     keep.start()
+    pl.semaphore_wait(row_ready, side - 1)
     sums = []
-    for d in range(1, planes):
-        rows = pl.ds(pl.multiple_of(16 * plane_head(d), 16), 16)
+    for i, step in enumerate(steps):
+        target = plane_head(step)
+        rows = pl.ds(pl.multiple_of(16 * target, 16), 16)
         sums.append(
-            send(rs_out.at[rows], sum_h.at[h], sum_ss.at[d - 1], sum_rs.at[d - 1], (c, plane_head(d)))
+            send(rs_out.at[rows], sum_h.at[h], sum_ss.at[i], sum_rs.at[i], (c, target))
         )
 
     inter = jnp.zeros((HEADS, ROWS), F32)
@@ -542,6 +618,14 @@
 
     for copy in sends:
         copy.wait_send()
+
+    @pl.when(middle)
+    def _():
+        relay.wait_send()
+
+    @pl.when(upper_half)
+    def _():
+        direct.wait_send()
 
 
 def finish(a_in, a_sum, a_dec, o_in, o_b, o_c, o_dec, wide, sums, both, decay, load, store):
@@ -636,14 +720,17 @@
             dma((2,)),
             dma((CUBE - 1,)),
             dma((CUBE - 1,)),
-            dma((groups - 1,)),
-            dma((groups - 1,)),
+            dma((4,)),
+            dma((3,)),
             dma((CUBE - 1,)),
             dma((CUBE - 1,)),
             dma((CUBE,)),
             dma((CUBE,)),
             dma((max(planes - 1, 1),)),
             dma((max(planes - 1, 1),)),
+            pltpu.SemaphoreType.REGULAR,
+            pltpu.SemaphoreType.REGULAR,
+            pltpu.SemaphoreType.REGULAR,
             pltpu.SemaphoreType.REGULAR,
             dma((9,)),
             dma((6,)),

time: 47.8 us -> 46.7 us (0.977)
  Pallas kernels: 47 us -> 45.9 us
    pallas_call x1, Pallas kernels: 45.1 us -> 44 us  [body(): pl.pallas_call(functools.partial(kernel, chips, planes), out_shape=(jax.S...]
where the time goes in v3:
time: 46.7 us; the launch traced here: 46.6 us
  Pallas kernels  45.9 us (98%)
  between operations  0.64 us (1%)
    pallas_call x1, Pallas kernels, body(): pl.pallas_call(functools.partial(kernel, chips, planes), out_shape=(jax.S...  44 us
    pallas_call x1, Pallas kernels, body(): pl.pallas_call(finish, out_shape=(jax.ShapeDtypeStruct((ROWS, WIDE), F32)...  1.89 us

profile of v3, /device:TPU:1, one launch (start us, length us, event | category | flops | bytes accessed | tf_op | source)
XLA Modules:
  0.0 46.6 jit_solution(11289592919428643909)
XLA Ops:
  0.6 44.0 %layer.1 = (f32[256,512]{1,0:T(8,128)}, bf16[16,16,256]{2,1,0:T(8,128)(2,1)}, f32[8,256]{1,0:T(8,128)}) custom-call(bf16[256,512]{1,0:T(8,128)(2,1)} %tok_h.1, s32[1,256]{1,0:T(1,128)} %bitcast.4, f32[8,256]{1,0:T(8,128)} %log_h.1, bf16[256,128]{1,0:T(8,128)(2,1)} %bp_h.1, bf16[256,128]{1,0:T(8,128)(2,1)} %cp_h.1, bf16[256,512]{1,0:T(8,128)(2,1)} %gr_h.1, ...), custom_call_target="tpu_custom_call" | custom-call | tf_op jit(solution)/shard_map/layer/pallas_call | solution.py:667
  44.7 1.9 %finish.1 = (f32[256,512]{1,0:T(8,128)}, f32[16,128]{1,0:T(8,128)}, f32[16,128]{1,0:T(8,128)}, f32[8,256]{1,0:T(8,128)}) custom-call(f32[256,512]{1,0:T(8,128)} %get-tuple-element.7.a_in, bf16[16,16,256]{2,1,0:T(8,128)(2,1)} %get-tuple-element.8.a_sum, f32[8,256]{1,0:T(8,128)} %get-tuple-element.9.a_dec), custom_call_target="tpu_custom_call" | custom-call | tf_op jit(solution)/shard_map/finish/pallas_call | solution.py:753

commit v4 on v3

--- a/solution.py
+++ b/solution.py
@@ -140,6 +140,7 @@
     l2,
     o3,
     full,
+    into,
     rs_src,
     rs_out,
     halo_s,
@@ -529,8 +530,6 @@
         slot = full.at[core, in_cube(CUBE - d)]
         forwards.append(send(slot, slot, fw_ss.at[d], fw_rs.at[d], partner))
     third.wait_recv()
-    for copy in forwards:
-        copy.wait_recv()
 
     def incoming(half, which):
         blocks = []
@@ -544,29 +543,28 @@
 
     late = (core == 1).astype(F32)
     early = 1.0 - late
-    state_in, adjoint_in, end_row = [], [], []
-    for half in range(2):
+
+    for half in (core, other):
+        if half is other:
+            for copy in forwards:
+                copy.wait_recv()
+        lanes = pl.ds(pl.multiple_of(256 * half, 256), 256)
         f_other = rx_full[half, STATE : STATE + 1]
         received = rx_full[half, 0:STATE]
-        f_own = loc[0, half, STATE : STATE + 1]
-        wide = incoming(half, 0)
-        state = late * received + (late * f_other + early) * wide
-        wide = incoming(half, 1)
-        adjoint = early * received + (early * f_other + late) * wide
-        state_out = loc[0, half, 0:STATE] + f_own * state
-        end_row.append(jnp.sum(adjoint * state_out, axis=0, keepdims=True))
-        state_in.append(split(state))
-        adjoint_in.append(split(adjoint))
-
-    b_part = rs_src[:, 0:STATE]
-    c_part = rs_src[:, STATE:]
-    for half in range(2):
-        lanes = slice(256 * half, 256 * half + 256)
-        for left, right in ((0, 0), (1, 0), (0, 1)):
-            b_part = b_part + dot(wact[left, :, lanes], adjoint_in[half][right], NT)
-            c_part = c_part + dot(wgr[left, :, lanes], state_in[half][right], NT)
-    rs_out[:, 0:STATE] = b_part.astype(BF16)
-    rs_out[:, STATE:] = c_part.astype(BF16)
+        state = late * received + (late * f_other + early) * incoming(half, 0)
+        adjoint = early * received + (early * f_other + late) * incoming(half, 1)
+        into[0, half] = state
+        into[1, half] = adjoint
+        for which, value, rows in ((0, adjoint, wact), (1, state, wgr)):
+            high, low = split(value)
+            both = dot(rows[0, :, lanes], jnp.concatenate([high, low], axis=0), NT)
+            part = both[:, 0:STATE] + both[:, STATE:] + dot(rows[1, :, lanes], high, NT)
+            columns = slice(STATE * which, STATE * which + STATE)
+            if half is other:
+                rs_out[:, columns] = (rs_src[:, columns] + part).astype(BF16)
+            else:
+                rs_src[:, columns] += part
+
     keep = pltpu.make_async_copy(
         rs_out.at[pl.ds(pl.multiple_of(16 * h, 16), 16)], sum_h.at[h], store.at[4]
     )
@@ -581,10 +579,14 @@
         )
 
     inter = jnp.zeros((HEADS, ROWS), F32)
+    end_row = []
     for half in range(2):
         lanes = slice(256 * half, 256 * half + 256)
-        after_part = wout[:, lanes] * dot(bp[...], adjoint_in[half][0])
-        before_part = win[:, lanes] * dot(cp[...], state_in[half][0])
+        state, adjoint = into[0, half], into[1, half]
+        state_out = loc[0, half, 0:STATE] + loc[0, half, STATE : STATE + 1] * state
+        end_row.append(jnp.sum(adjoint * state_out, axis=0, keepdims=True))
+        after_part = wout[:, lanes] * dot(bp[...], adjoint.astype(BF16))
+        before_part = win[:, lanes] * dot(cp[...], state.astype(BF16))
         pg[0:ROWS, lanes] = (agr[:, lanes] + after_part) * slope[:, lanes]
         difference = before_part * gr[:, lanes].astype(F32) - after_part * act[:, lanes].astype(F32)
         inter = inter + exact_dot(pick[:, lanes], difference, NT)
@@ -707,6 +709,7 @@
             vmem((groups, 80, 128), jnp.int16),
             vmem((CUBE, 144, 128), jnp.int16),
             vmem((2, CUBE, 144, 128), jnp.int16),
+            vmem((2, 2, STATE, 256), F32),
             vmem((ROWS, 2 * STATE), F32),
             vmem((ROWS, 2 * STATE), BF16),
             vmem((16, WIDE), BF16),

time: 46.7 us -> 46.6 us (level)
  no operation moved by 1% of the time
where the time goes in v4:
time: 46.6 us; the launch traced here: 46.4 us
  Pallas kernels  45.8 us (98%)
  between operations  0.64 us (1%)
    pallas_call x1, Pallas kernels, body(): pl.pallas_call(functools.partial(kernel, chips, planes), out_shape=(jax.S...  43.9 us
    pallas_call x1, Pallas kernels, body(): pl.pallas_call(finish, out_shape=(jax.ShapeDtypeStruct((ROWS, WIDE), F32)...  1.89 us

profile of v4, /device:TPU:1, one launch (start us, length us, event | category | flops | bytes accessed | tf_op | source)
XLA Modules:
  0.0 46.4 jit_solution(4366618886581187571)
XLA Ops:
  0.6 43.9 %layer.1 = (f32[256,512]{1,0:T(8,128)}, bf16[16,16,256]{2,1,0:T(8,128)(2,1)}, f32[8,256]{1,0:T(8,128)}) custom-call(bf16[256,512]{1,0:T(8,128)(2,1)} %tok_h.1, s32[1,256]{1,0:T(1,128)} %bitcast.4, f32[8,256]{1,0:T(8,128)} %log_h.1, bf16[256,128]{1,0:T(8,128)(2,1)} %bp_h.1, bf16[256,128]{1,0:T(8,128)(2,1)} %cp_h.1, bf16[256,512]{1,0:T(8,128)(2,1)} %gr_h.1, ...), custom_call_target="tpu_custom_call" | custom-call | tf_op jit(solution)/shard_map/layer/pallas_call | solution.py:669
  44.6 1.9 %finish.1 = (f32[256,512]{1,0:T(8,128)}, f32[16,128]{1,0:T(8,128)}, f32[16,128]{1,0:T(8,128)}, f32[8,256]{1,0:T(8,128)}) custom-call(f32[256,512]{1,0:T(8,128)} %get-tuple-element.7.a_in, bf16[16,16,256]{2,1,0:T(8,128)(2,1)} %get-tuple-element.8.a_sum, f32[8,256]{1,0:T(8,128)} %get-tuple-element.9.a_dec), custom_call_target="tpu_custom_call" | custom-call | tf_op jit(solution)/shard_map/finish/pallas_call | solution.py:756

commit v5 on v4

--- a/solution.py
+++ b/solution.py
@@ -237,7 +237,7 @@
         copy.start()
     sends = []
 
-    def send(src, dst, send_sem, recv_sem, device):
+    def send(src, dst, send_sem, recv_sem, device, now=True):
         copy = pltpu.make_async_remote_copy(
             src_ref=src,
             dst_ref=dst,
@@ -246,7 +246,8 @@
             device_id=device,
             device_id_type=MESH,
         )
-        copy.start()
+        if now:
+            copy.start()
         sends.append(copy)
         return copy
 
@@ -323,6 +324,21 @@
 
     pl.semaphore_wait(barrier, len(peers))
     halo = send(halo_s, halo_r, halo_ss.at[0], halo_rs.at[0], after)
+    first = send(
+        loc.at[core, other], rx_full.at[other], pair_ss.at[0], pair_rs.at[0], partner, now=False
+    )
+    second = send(
+        loc.at[other, other], rx_half, pair_ss.at[1], pair_rs.at[1], partner, now=False
+    )
+
+    @pl.when(core == 1)
+    def _():
+        first.start()
+
+    @pl.when(core == 0)
+    def _():
+        second.start()
+
     lowest, highest = place == 0, place == CUBE - 1
     for d in range(1, side):
         pl.semaphore_signal(row_ready, inc=1, device_id=(c, across(d)), device_id_type=MESH)
@@ -340,10 +356,14 @@
     for half in range(2):
         loc[0, half, 0:STATE] += local_state(slice(0, 16), half)
 
-    first = send(
-        loc.at[core, other], rx_full.at[other], pair_ss.at[0], pair_rs.at[0], partner
-    )
-    second = send(loc.at[other, other], rx_half, pair_ss.at[1], pair_rs.at[1], partner)
+    @pl.when(core == 0)
+    def _():
+        first.start()
+
+    @pl.when(core == 1)
+    def _():
+        second.start()
+
     third = send(loc.at[core, core], rx_full.at[core], pair_ss.at[2], pair_rs.at[2], partner)
 
     @pl.when(lowest | highest)

time: 46.6 us -> 46.4 us (level)
  no operation moved by 1% of the time
where the time goes in v5:
time: 46.4 us; the launch traced here: 46.2 us
  Pallas kernels  45.6 us (98%)
  between operations  0.64 us (1%)
    pallas_call x1, Pallas kernels, body(): pl.pallas_call(functools.partial(kernel, chips, planes), out_shape=(jax.S...  43.7 us
    pallas_call x1, Pallas kernels, body(): pl.pallas_call(finish, out_shape=(jax.ShapeDtypeStruct((ROWS, WIDE), F32)...  1.89 us

profile of v5, /device:TPU:1, one launch (start us, length us, event | category | flops | bytes accessed | tf_op | source)
XLA Modules:
  0.0 46.2 jit_solution(16464501879510442749)
XLA Ops:
  0.6 43.7 %layer.1 = (f32[256,512]{1,0:T(8,128)}, bf16[16,16,256]{2,1,0:T(8,128)(2,1)}, f32[8,256]{1,0:T(8,128)}) custom-call(bf16[256,512]{1,0:T(8,128)(2,1)} %tok_h.1, s32[1,256]{1,0:T(1,128)} %bitcast.4, f32[8,256]{1,0:T(8,128)} %log_h.1, bf16[256,128]{1,0:T(8,128)(2,1)} %bp_h.1, bf16[256,128]{1,0:T(8,128)(2,1)} %cp_h.1, bf16[256,512]{1,0:T(8,128)(2,1)} %gr_h.1, ...), custom_call_target="tpu_custom_call" | custom-call | tf_op jit(solution)/shard_map/layer/pallas_call | solution.py:689
  44.4 1.9 %finish.1 = (f32[256,512]{1,0:T(8,128)}, f32[16,128]{1,0:T(8,128)}, f32[16,128]{1,0:T(8,128)}, f32[8,256]{1,0:T(8,128)}) custom-call(f32[256,512]{1,0:T(8,128)} %get-tuple-element.7.a_in, bf16[16,16,256]{2,1,0:T(8,128)(2,1)} %get-tuple-element.8.a_sum, f32[8,256]{1,0:T(8,128)} %get-tuple-element.9.a_dec), custom_call_target="tpu_custom_call" | custom-call | tf_op jit(solution)/shard_map/finish/pallas_call | solution.py:776
